TPU v7x, 32 devices: a whole 2x2x4 slice. The times are simulated.
32 devices in a mesh: wide: 8 (over z, y), narrow: 4 (over x, core).
Axes of the slice: x: 2, y: 2, z: 4, core: 2. Of those that a mesh axis runs over, the one named last changes fastest.
Arguments:
- images: bfloat16 [8192, 1152], P(('wide', 'narrow')), may hold values from -0.1875 to 0.1875
- texts: bfloat16 [8192, 1152], P(('wide', 'narrow')), may hold values from -0.1875 to 0.1875
- labels: int32 [8192], P(('wide', 'narrow')), may hold values from 0 to 8191, as said below
- log_scale: float32 [1], replicated, may hold values from 1 to 2.3
- bias: float32 [1], replicated, may hold values from -4 to -2
Outputs:
- grad_images: float32 [8192, 1152], P(('wide', 'narrow'))
- grad_texts: float32 [8192, 1152], P(('wide', 'narrow'))
Inputs may be any that keep to these rules, and one draw needn't show every extreme that they name: labels_i names a text row of the same block of 256 rows as row i, and the labels of each block are a permutation of that block's rows.
All inputs are finite; a program needn't handle non-finite values.
Results may differ from a plain program's by a relative error of at most 0.0042.
Values may be sent and summed in bfloat16 or wider, within the bound.
A program may use at most 64 MiB of HBM per device.

v0:
```python
import jax
import jax.numpy as jnp
from jax import lax
from jax.sharding import PartitionSpec as P

WINDOW = 4


EPS = 1e-06


def shifted(value, axis, steps):
    count = lax.axis_size(axis)
    pairs = [(source, (source + steps) % count) for source in range(count)]
    return lax.ppermute(value, axis, pairs)


def normalize(vectors):
    floats = vectors.astype(jnp.float32)
    inverse = lax.rsqrt(jnp.sum(floats * floats, axis=-1, keepdims=True) + EPS)
    return (floats * inverse, inverse)


def unit_backward(unit_rows, inverse, upstream):
    return inverse * (upstream - unit_rows * jnp.sum(unit_rows * upstream, axis=-1, keepdims=True))


def shortest(distance, count):
    remain = distance % count
    return remain if remain <= count // 2 else remain - count


def weigh_block(image_rows, text_rows, row_labels, target, temper, offset):
    scores = jnp.einsum("id,jd->ij", image_rows, text_rows, preferred_element_type=jnp.float32)
    logits = temper * scores + offset
    positive = (row_labels[:, None] == target[None, :]).astype(jnp.float32)
    residual = jax.nn.sigmoid(logits) - positive
    return (temper * residual).astype(jnp.bfloat16)


def image_side(image_grad, visitor, image_half, labels, temper, offset, anchor):
    block_rows = visitor.shape[0]
    target = anchor * block_rows + jnp.arange(block_rows, dtype=jnp.int32)
    weighted = weigh_block(image_half, visitor, labels, target, temper, offset)
    image_grad = image_grad + jnp.dot(weighted, visitor, preferred_element_type=jnp.float32)
    return (image_grad, weighted)


def visit(image_grad, visitor, carried, image_half, labels, temper, offset, anchor):
    image_grad, weighted = image_side(
        image_grad, visitor, image_half, labels, temper, offset, anchor
    )
    carried = carried + jnp.einsum(
        "ij,id->jd", weighted, image_half, preferred_element_type=jnp.float32
    )
    return (image_grad, carried)


def shards(images, texts, labels, log_scale, bias):
    image_unit, image_inverse = normalize(images)
    text_unit, text_inverse = normalize(texts)
    image_half = image_unit.astype(jnp.bfloat16)
    text_half = text_unit.astype(jnp.bfloat16)
    temper = jnp.exp(log_scale[0])
    offset = bias[0]
    wide_count = lax.axis_size("wide")
    narrow_count = lax.axis_size("narrow")
    wide_index = lax.axis_index("wide")
    narrow_index = lax.axis_index("narrow")

    def source(wide_back, narrow_back):
        return (wide_index - wide_back) % wide_count * narrow_count + (
            narrow_index - narrow_back
        ) % narrow_count

    image_grad = jnp.zeros(images.shape, jnp.float32)
    visitor = text_half
    carried = jnp.zeros(images.shape, jnp.float32)
    for number in range(2 * WINDOW):
        wide_back = number // WINDOW
        narrow_back = number - wide_back * WINDOW + wide_back * (WINDOW - 1)
        image_grad, carried = visit(
            image_grad,
            visitor,
            carried,
            image_half,
            labels,
            temper,
            offset,
            source(wide_back, narrow_back),
        )
        if number == WINDOW - 1:
            visitor = shifted(visitor, "wide", 1)
            carried = shifted(carried, "wide", 1)
        elif number < 2 * WINDOW - 1:
            visitor = shifted(visitor, "narrow", 1)
            carried = shifted(carried, "narrow", 1)
    carried = shifted(carried, "wide", -1)
    return_hop = shortest(-(2 * WINDOW - 2), narrow_count)
    carried = shifted(carried, "narrow", return_hop)
    grad_images = unit_backward(image_unit, image_inverse, image_grad)
    grad_texts = unit_backward(text_unit, text_inverse, carried)
    return (grad_images, grad_texts)


def solution(mesh):
    return jax.shard_map(
        shards,
        mesh=mesh,
        in_specs=(
            P(("wide", "narrow"), None),
            P(("wide", "narrow"), None),
            P(("wide", "narrow")),
            P(),
            P(),
        ),
        out_specs=(P(("wide", "narrow"), None), P(("wide", "narrow"), None)),
        check_vma=False,
    )
```

profile of v0, /device:TPU:0, one launch (start us, length us, event | category | flops | bytes accessed | tf_op | source)
XLA Modules:
  0.0 252.6 jit_solution(449425920012655257)
XLA Ops:
  6.2 2.6 %collective-permute-start = (bf16[256,1152]{1,0:T(8,128)(2,1)S(1)}, bf16[256,1152]{1,0:T(8,128)(2,1)S(1)}, u32[]{:S(2)}, u32[]{:S(2)}) collective-permute-start(bf16[256,1152]{1,0:T(8,128)(2,1)S(1)} %fusion.2), channel_id=1, source_target_pairs={{0,1},{1,2},{2,3},{3,0},{4,5},{5,6},{6,7},{7,4},{8,9},{9,10},{10,1... | collective-permute-start | bytes 1769480 | tf_op jit(solution)/shard_map/ppermute | solution.py:15
  8.8 19.5 %collective-permute-done = bf16[256,1152]{1,0:T(8,128)(2,1)S(1)} collective-permute-done((bf16[256,1152]{1,0:T(8,128)(2,1)S(1)}, bf16[256,1152]{1,0:T(8,128)(2,1)S(1)}, u32[]{:S(2)}, u32[]{:S(2)}) %collective-permute-start) | collective-permute-done | bytes 589856 | tf_op jit(solution)/shard_map/ppermute | solution.py:15
  28.8 1.7 convolution_add_fusion
  30.6 2.4 collective-permute-start.1
  33.0 19.6 %collective-permute-done.1 = bf16[256,1152]{1,0:T(8,128)(2,1)} collective-permute-done((bf16[256,1152]{1,0:T(8,128)(2,1)S(1)}, bf16[256,1152]{1,0:T(8,128)(2,1)}, u32[]{:S(2)}, u32[]{:S(2)}) %collective-permute-start.1) | collective-permute-done | bytes 589856 | tf_op jit(solution)/shard_map/ppermute | solution.py:15
  52.7 1.5 fusion.72
  56.3 2.4 collective-permute-start.2
  58.7 19.6 %collective-permute-done.2 = bf16[256,1152]{1,0:T(8,128)(2,1)} collective-permute-done((bf16[256,1152]{1,0:T(8,128)(2,1)}, bf16[256,1152]{1,0:T(8,128)(2,1)}, u32[]{:S(2)}, u32[]{:S(2)}) %collective-permute-start.2) | collective-permute-done | bytes 589856 | tf_op jit(solution)/shard_map/ppermute | solution.py:15
  78.3 1.5 fusion.73
  81.9 2.4 collective-permute-start.10
  84.3 1.5 collective-permute-start.3
  85.8 39.5 %collective-permute-done.3 = bf16[256,1152]{1,0:T(8,128)(2,1)} collective-permute-done((bf16[256,1152]{1,0:T(8,128)(2,1)}, bf16[256,1152]{1,0:T(8,128)(2,1)}, u32[]{:S(2)}, u32[]{:S(2)}) %collective-permute-start.3) | collective-permute-done | bytes 589856 | tf_op jit(solution)/shard_map/ppermute | solution.py:15
  125.3 1.5 fusion.74
  129.6 21.4 %collective-permute-done.4 = bf16[256,1152]{1,0:T(8,128)(2,1)} collective-permute-done((bf16[256,1152]{1,0:T(8,128)(2,1)}, bf16[256,1152]{1,0:T(8,128)(2,1)}, u32[]{:S(2)}, u32[]{:S(2)}) %collective-permute-start.4) | collective-permute-done | bytes 589856 | tf_op jit(solution)/shard_map/ppermute | solution.py:15
  151.0 1.5 fusion.75
  155.3 21.4 %collective-permute-done.5 = bf16[256,1152]{1,0:T(8,128)(2,1)} collective-permute-done((bf16[256,1152]{1,0:T(8,128)(2,1)}, bf16[256,1152]{1,0:T(8,128)(2,1)}, u32[]{:S(2)}, u32[]{:S(2)}) %collective-permute-start.5) | collective-permute-done | bytes 589856 | tf_op jit(solution)/shard_map/ppermute | solution.py:15
  176.6 1.5 fusion.76
  181.5 4.7 %collective-permute-done.6 = bf16[256,1152]{1,0:T(8,128)(2,1)S(1)} collective-permute-done((bf16[256,1152]{1,0:T(8,128)(2,1)}, bf16[256,1152]{1,0:T(8,128)(2,1)S(1)}, u32[]{:S(2)}, u32[]{:S(2)}) %collective-permute-start.6) | collective-permute-done | bytes 589856 | tf_op jit(solution)/shard_map/ppermute | solution.py:15
  187.0 11.8 %collective-permute-done.13 = f32[256,1152]{1,0:T(8,128)S(1)} collective-permute-done((f32[256,1152]{1,0:T(8,128)S(1)}, f32[256,1152]{1,0:T(8,128)S(1)}, u32[]{:S(2)}, u32[]{:S(2)}) %collective-permute-start.13) | collective-permute-done | bytes 1179680 | tf_op jit(solution)/shard_map/ppermute | solution.py:15
  198.9 2.0 collective-permute-start.14
  203.8 1.4 convolution_add_fusion.4
  206.7 18.5 %collective-permute-done.14 = f32[256,1152]{1,0:T(8,128)S(1)} collective-permute-done((f32[256,1152]{1,0:T(8,128)S(1)}, f32[256,1152]{1,0:T(8,128)S(1)}, u32[]{:S(2)}, u32[]{:S(2)}) %collective-permute-start.14) | collective-permute-done | bytes 1179680 | tf_op jit(solution)/shard_map/ppermute | solution.py:15
  225.2 1.5 collective-permute-start.15
  229.8 21.1 %collective-permute-done.15 = f32[256,1152]{1,0:T(8,128)S(1)} collective-permute-done((f32[256,1152]{1,0:T(8,128)S(1)}, f32[256,1152]{1,0:T(8,128)S(1)}, u32[]{:S(2)}, u32[]{:S(2)}) %collective-permute-start.15) | collective-permute-done | bytes 1179680 | tf_op jit(solution)/shard_map/ppermute | solution.py:15
  (84 shorter events, 27.6 us)
Async XLA Ops:
  0.6 2.7 %copy-start.1 = (bf16[256,1152]{1,0:T(8,128)(2,1)S(1)}, bf16[256,1152]{1,0:T(8,128)(2,1)}, u32[]{:S(2)}) copy-start(bf16[256,1152]{1,0:T(8,128)(2,1)} %param.6) | copy-start | bytes 1769476
  0.7 4.2 %copy-start = (bf16[256,1152]{1,0:T(8,128)(2,1)S(1)}, bf16[256,1152]{1,0:T(8,128)(2,1)}, u32[]{:S(2)}) copy-start(bf16[256,1152]{1,0:T(8,128)(2,1)} %param.5) | copy-start | bytes 1769476
  0.7 4.2 %copy-start.14 = (s32[256]{0:T(256)S(1)}, s32[256]{0:T(256)}, u32[]{:S(2)}) copy-start(s32[256]{0:T(256)} %param.7) | copy-start | bytes 3076
  5.7 23.1 %collective-permute-start.7 = (f32[256,1152]{1,0:T(8,128)S(1)}, f32[256,1152]{1,0:T(8,128)}, u32[]{:S(2)}, u32[]{:S(2)}) collective-permute-start(f32[256,1152]{1,0:T(8,128)S(1)} %fusion.91), channel_id=1, source_target_pairs={{0,1},{1,2},{2,3},{3,0},{4,5},{5,6},{6,7},{7,4},{8,9},{9,10},{10,1... | collective-permute-start | bytes 3538952 | tf_op jit(solution)/shard_map/ppermute | solution.py:15
  6.2 22.1 %collective-permute-start = (bf16[256,1152]{1,0:T(8,128)(2,1)S(1)}, bf16[256,1152]{1,0:T(8,128)(2,1)S(1)}, u32[]{:S(2)}, u32[]{:S(2)}) collective-permute-start(bf16[256,1152]{1,0:T(8,128)(2,1)S(1)} %fusion.2), channel_id=1, source_target_pairs={{0,1},{1,2},{2,3},{3,0},{4,5},{5,6},{6,7},{7,4},{8,9},{9,10},{10,1... | collective-permute-start | bytes 1769480 | tf_op jit(solution)/shard_map/ppermute | solution.py:15
  28.8 1.8 copy-start.2
  30.6 24.2 %collective-permute-start.8 = (f32[256,1152]{1,0:T(8,128)S(1)}, f32[256,1152]{1,0:T(8,128)}, u32[]{:S(2)}, u32[]{:S(2)}) collective-permute-start(f32[256,1152]{1,0:T(8,128)S(1)} %convolution_add_fusion), channel_id=1, source_target_pairs={{0,1},{1,2},{2,3},{3,0},{4,5},{5,6},{6,7},{7,4},{8,9},{9,10},{10,1... | collective-permute-start | bytes 3538952 | tf_op jit(solution)/shard_map/ppermute | solution.py:15
  30.6 22.0 %collective-permute-start.1 = (bf16[256,1152]{1,0:T(8,128)(2,1)S(1)}, bf16[256,1152]{1,0:T(8,128)(2,1)}, u32[]{:S(2)}, u32[]{:S(2)}) collective-permute-start(bf16[256,1152]{1,0:T(8,128)(2,1)S(1)} %collective-permute-done), channel_id=1, source_target_pairs={{0,1},{1,2},{2,3},{3,0},{4,5},{5,6},{6,7},{7,4},{8,9},{9,10},{10,1... | collective-permute-start | bytes 1769480 | tf_op jit(solution)/shard_map/ppermute | solution.py:15
  56.2 24.3 %collective-permute-start.9 = (f32[256,1152]{1,0:T(8,128)S(1)}, f32[256,1152]{1,0:T(8,128)}, u32[]{:S(2)}, u32[]{:S(2)}) collective-permute-start(f32[256,1152]{1,0:T(8,128)S(1)} %add.322), channel_id=1, source_target_pairs={{0,1},{1,2},{2,3},{3,0},{4,5},{5,6},{6,7},{7,4},{8,9},{9,10},{10,1... | collective-permute-start | bytes 3538952 | tf_op jit(solution)/shard_map/ppermute | solution.py:15
  56.3 22.0 %collective-permute-start.2 = (bf16[256,1152]{1,0:T(8,128)(2,1)}, bf16[256,1152]{1,0:T(8,128)(2,1)}, u32[]{:S(2)}, u32[]{:S(2)}) collective-permute-start(bf16[256,1152]{1,0:T(8,128)(2,1)} %collective-permute-done.1), channel_id=1, source_target_pairs={{0,1},{1,2},{2,3},{3,0},{4,5},{5,6},{6,7},{7,4},{8,9},{9,10},{10,1... | collective-permute-start | bytes 1769480 | tf_op jit(solution)/shard_map/ppermute | solution.py:15
  81.9 45.6 %collective-permute-start.10 = (f32[256,1152]{1,0:T(8,128)S(1)}, f32[256,1152]{1,0:T(8,128)}, u32[]{:S(2)}, u32[]{:S(2)}) collective-permute-start(f32[256,1152]{1,0:T(8,128)S(1)} %add.323), channel_id=1, source_target_pairs={{0,4},{4,8},{8,12},{12,16},{16,20},{20,24},{24,28},{28,0},{1,5},{5... | collective-permute-start | bytes 3538952 | tf_op jit(solution)/shard_map/ppermute | solution.py:15
  84.3 41.0 %collective-permute-start.3 = (bf16[256,1152]{1,0:T(8,128)(2,1)}, bf16[256,1152]{1,0:T(8,128)(2,1)}, u32[]{:S(2)}, u32[]{:S(2)}) collective-permute-start(bf16[256,1152]{1,0:T(8,128)(2,1)} %collective-permute-done.2), channel_id=1, source_target_pairs={{0,4},{4,8},{8,12},{12,16},{16,20},{20,24},{24,28},{28,0},{1,5},{5... | collective-permute-start | bytes 1769480 | tf_op jit(solution)/shard_map/ppermute | solution.py:15
  128.9 24.2 %collective-permute-start.11 = (f32[256,1152]{1,0:T(8,128)S(1)}, f32[256,1152]{1,0:T(8,128)}, u32[]{:S(2)}, u32[]{:S(2)}) collective-permute-start(f32[256,1152]{1,0:T(8,128)S(1)} %add.324), channel_id=1, source_target_pairs={{0,1},{1,2},{2,3},{3,0},{4,5},{5,6},{6,7},{7,4},{8,9},{9,10},{10,1... | collective-permute-start | bytes 3538952 | tf_op jit(solution)/shard_map/ppermute | solution.py:15
  128.9 22.0 %collective-permute-start.4 = (bf16[256,1152]{1,0:T(8,128)(2,1)}, bf16[256,1152]{1,0:T(8,128)(2,1)}, u32[]{:S(2)}, u32[]{:S(2)}) collective-permute-start(bf16[256,1152]{1,0:T(8,128)(2,1)} %collective-permute-done.3), channel_id=1, source_target_pairs={{0,1},{1,2},{2,3},{3,0},{4,5},{5,6},{6,7},{7,4},{8,9},{9,10},{10,1... | collective-permute-start | bytes 1769480 | tf_op jit(solution)/shard_map/ppermute | solution.py:15
  154.5 24.0 %collective-permute-start.12 = (f32[256,1152]{1,0:T(8,128)S(1)}, f32[256,1152]{1,0:T(8,128)}, u32[]{:S(2)}, u32[]{:S(2)}) collective-permute-start(f32[256,1152]{1,0:T(8,128)S(1)} %add.325), channel_id=1, source_target_pairs={{0,1},{1,2},{2,3},{3,0},{4,5},{5,6},{6,7},{7,4},{8,9},{9,10},{10,1... | collective-permute-start | bytes 3538952 | tf_op jit(solution)/shard_map/ppermute | solution.py:15
  154.6 22.0 %collective-permute-start.5 = (bf16[256,1152]{1,0:T(8,128)(2,1)}, bf16[256,1152]{1,0:T(8,128)(2,1)}, u32[]{:S(2)}, u32[]{:S(2)}) collective-permute-start(bf16[256,1152]{1,0:T(8,128)(2,1)} %collective-permute-done.4), channel_id=1, source_target_pairs={{0,1},{1,2},{2,3},{3,0},{4,5},{5,6},{6,7},{7,4},{8,9},{9,10},{10,1... | collective-permute-start | bytes 1769480 | tf_op jit(solution)/shard_map/ppermute | solution.py:15
  176.6 9.5 %collective-permute-start.6 = (bf16[256,1152]{1,0:T(8,128)(2,1)}, bf16[256,1152]{1,0:T(8,128)(2,1)S(1)}, u32[]{:S(2)}, u32[]{:S(2)}) collective-permute-start(bf16[256,1152]{1,0:T(8,128)(2,1)} %collective-permute-done.5), channel_id=1, source_target_pairs={{0,1},{1,2},{2,3},{3,0},{4,5},{5,6},{6,7},{7,4},{8,9},{9,10},{10,1... | collective-permute-start | bytes 1769480 | tf_op jit(solution)/shard_map/ppermute | solution.py:15
  178.5 2.2 copy-start.13
  180.0 18.8 %collective-permute-start.13 = (f32[256,1152]{1,0:T(8,128)S(1)}, f32[256,1152]{1,0:T(8,128)S(1)}, u32[]{:S(2)}, u32[]{:S(2)}) collective-permute-start(f32[256,1152]{1,0:T(8,128)S(1)} %add.326), channel_id=1, source_target_pairs={{0,1},{1,2},{2,3},{3,0},{4,5},{5,6},{6,7},{7,4},{8,9},{9,10},{10,1... | collective-permute-start | bytes 3538952 | tf_op jit(solution)/shard_map/ppermute | solution.py:15
  187.0 13.9 %copy-start.5 = (bf16[256,256]{1,0:T(8,128)(2,1)S(1)}, bf16[256,256]{1,0:T(8,128)(2,1)}, u32[]{:S(2)}) copy-start(bf16[256,256]{1,0:T(8,128)(2,1)} %copy-done.4) | copy-start | bytes 393220
  198.9 3.4 %copy-start.7 = (bf16[256,256]{1,0:T(8,128)(2,1)S(1)}, bf16[256,256]{1,0:T(8,128)(2,1)}, u32[]{:S(2)}) copy-start(bf16[256,256]{1,0:T(8,128)(2,1)} %copy-done.6) | copy-start | bytes 393220
  198.9 26.3 %collective-permute-start.14 = (f32[256,1152]{1,0:T(8,128)S(1)}, f32[256,1152]{1,0:T(8,128)S(1)}, u32[]{:S(2)}, u32[]{:S(2)}) collective-permute-start(f32[256,1152]{1,0:T(8,128)S(1)} %add.327), channel_id=1, source_target_pairs={{0,28},{4,0},{8,4},{12,8},{16,12},{20,16},{24,20},{28,24},{1,29},{... | collective-permute-start | bytes 3538952 | tf_op jit(solution)/shard_map/ppermute | solution.py:15
  203.8 1.5 copy-start.11
  225.2 25.8 %collective-permute-start.15 = (f32[256,1152]{1,0:T(8,128)S(1)}, f32[256,1152]{1,0:T(8,128)S(1)}, u32[]{:S(2)}, u32[]{:S(2)}) collective-permute-start(f32[256,1152]{1,0:T(8,128)S(1)} %collective-permute-done.14), channel_id=1, source_target_pairs={{0,2},{1,3},{2,0},{3,1},{4,6},{5,7},{6,4},{7,5},{8,10},{9,11},{10,... | collective-permute-start | bytes 3538952 | tf_op jit(solution)/shard_map/ppermute | solution.py:15
  (7 other events, 6.2 us)
where the time goes:
time: 253 us
  waiting for transfers between devices  197 us (78%)
  matrix products  21.6 us (9%)
  starting transfers between devices  17.6 us (7%)
  other arithmetic  12.8 us (5%)
    ppermute x16, waiting for transfers between devices, shifted(): return lax.ppermute(value, axis, pairs)  197 us
    ppermute x16, starting transfers between devices, shifted(): return lax.ppermute(value, axis, pairs)  17.6 us
    dot_general x8, matrix products, weigh_block(): jnp.einsum('id,jd->ij', image_rows, text_rows, preferred_element_type=jnp...  8.7 us
    dot_general x8, matrix products, image_side(): jnp.dot(weighted, visitor, preferred_element_type=jnp.float32)  8.27 us
    add x6, other arithmetic, visit(): carried + jnp.einsum('ij,id->jd', weighted, image_half, preferred_element...  7.12 us
  transfers between devices with their start and end apart: 16, of which 10 were waited for; matrix products, arithmetic and copies ran while one was open for 9% of the time, Pallas kernels for 0%

commit v1 on v0

v1 whole, which is shorter than its diff:
```python
import functools

import jax
import jax.numpy as jnp
from jax import lax
from jax.experimental import pallas as pl
from jax.experimental.pallas import tpu as pltpu
from jax.sharding import PartitionSpec as P

WINDOW = 4
EPS = 1e-06
CHUNKS = 4
IMAGE, TEXT = 0, 1
MESH = pl.DeviceIdType.MESH


def normalize(vectors):
    floats = vectors.astype(jnp.float32)
    inverse = lax.rsqrt(jnp.sum(floats * floats, axis=-1, keepdims=True) + EPS)
    return (floats * inverse, inverse)


def unit_backward(unit_rows, inverse, upstream):
    return inverse * (upstream - unit_rows * jnp.sum(unit_rows * upstream, axis=-1, keepdims=True))


def kernel(
    wide_count,
    narrow_count,
    log_scale_ref,
    bias_ref,
    images_ref,
    texts_ref,
    labels_ref,
    grad_images_ref,
    grad_texts_ref,
    blocks,
    grads,
    send_sem,
    recv_sem,
):
    rows = blocks.shape[2]
    piece = rows // CHUNKS
    wide = lax.axis_index("wide")
    narrow = lax.axis_index("narrow")
    relay = narrow_count == WINDOW

    def device(wide_step, narrow_index):
        return (lax.rem(wide + wide_step + wide_count, wide_count), narrow_index)

    if relay:
        partner = device(0, narrow + 1 - 2 * lax.rem(narrow, 2))
        across = device(0, lax.rem(narrow + 2, narrow_count))
        onward = {IMAGE: device(-1, narrow), TEXT: device(1, narrow)}
        neighbours = [partner, across, onward[IMAGE], onward[TEXT]]
    else:
        direct = {}
        for side, sign in ((IMAGE, -1), (TEXT, 1)):
            for slot in range(1, 2 * WINDOW):
                wide_back = slot // WINDOW
                narrow_back = slot - wide_back * WINDOW + wide_back * (WINDOW - 1)
                index = lax.rem(narrow + sign * narrow_back + narrow_count, narrow_count)
                direct[side, slot] = device(sign * wide_back, index)
        neighbours = list(direct.values())

    barrier = pltpu.get_barrier_semaphore()
    for neighbour in neighbours:
        pl.semaphore_signal(barrier, inc=1, device_id=neighbour, device_id_type=MESH)

    temper = jnp.exp(jnp.full((1, rows), log_scale_ref[0], jnp.float32))
    offset = bias_ref[0]
    sources = {IMAGE: images_ref, TEXT: texts_ref}
    started = []

    def part(chunk):
        return pl.ds(chunk * piece, piece)

    def message(side, source_slot, slot, chunk, target):
        return pltpu.make_async_remote_copy(
            src_ref=blocks.at[side, source_slot, part(chunk)],
            dst_ref=blocks.at[side, slot, part(chunk)],
            send_sem=send_sem.at[side, slot, chunk],
            recv_sem=recv_sem.at[side, slot, chunk],
            device_id=target,
            device_id_type=MESH,
        )

    def send(side, source_slot, slot, chunk, target):
        copy = message(side, source_slot, slot, chunk, target)
        copy.start()
        started.append(copy)

    def arrived(side, slot, chunk):
        message(side, slot, slot, chunk, neighbours[0]).wait_recv()

    for chunk in range(CHUNKS):
        for side in (IMAGE, TEXT):
            unit, _ = normalize(sources[side][part(chunk), :])
            blocks[side, 0, part(chunk), :] = unit.astype(jnp.bfloat16)
        if chunk == 0:
            pl.semaphore_wait(barrier, len(neighbours))
        for side in (IMAGE, TEXT):
            if relay:
                send(side, 0, 2, chunk, across)
                send(side, 0, 4, chunk, onward[side])
                send(side, 0, 1, chunk, partner)
            else:
                for slot in range(1, 2 * WINDOW):
                    send(side, 0, slot, chunk, direct[side, slot])

    def residual(own, visitor):
        scores = lax.dot_general(
            own, visitor, (((1,), (1,)), ((), ())), preferred_element_type=jnp.float32
        )
        return jax.nn.sigmoid(temper * scores + offset)

    base = (wide * narrow_count + narrow) * rows
    target = base + lax.broadcasted_iota(jnp.int32, (rows, rows), 0)
    positive = (labels_ref[...] == target).astype(jnp.float32)
    weighted = (temper * (residual(blocks[TEXT, 0], blocks[IMAGE, 0]) - positive)).astype(jnp.bfloat16)
    grads[TEXT] = jnp.dot(weighted, blocks[IMAGE, 0], preferred_element_type=jnp.float32)
    grads[IMAGE] = lax.dot_general(
        weighted, blocks[TEXT, 0], (((0,), (0,)), ((), ())), preferred_element_type=jnp.float32
    )

    def visit(first, last):
        count = last - first

        @pl.loop(0, 2 * count)
        def _(step):
            side = lax.rem(step, 2)
            slot = first + step // 2
            own = 1 - side
            visitor = blocks[side, slot]
            weighted = (temper * residual(blocks[own, 0], visitor)).astype(jnp.bfloat16)
            grads[own] += jnp.dot(weighted, visitor, preferred_element_type=jnp.float32)

    if relay:
        for chunk in range(CHUNKS):
            for side in (IMAGE, TEXT):
                arrived(side, 1, chunk)
        visit(1, 2)
        for chunk in range(CHUNKS):
            arrived(IMAGE, 2, chunk)
            send(IMAGE, 2, 6, chunk, onward[IMAGE])
            send(IMAGE, 2, 3, chunk, partner)
            arrived(TEXT, 4, chunk)
            send(TEXT, 4, 6, chunk, across)
            send(TEXT, 4, 5, chunk, partner)
            arrived(TEXT, 2, chunk)
            send(TEXT, 2, 3, chunk, partner)
            arrived(IMAGE, 4, chunk)
            send(IMAGE, 4, 5, chunk, partner)
        for chunk in range(CHUNKS):
            for side in (IMAGE, TEXT):
                arrived(side, 3, chunk)
                arrived(side, 5, chunk)
        visit(2, 6)
        for chunk in range(CHUNKS):
            for side in (IMAGE, TEXT):
                arrived(side, 6, chunk)
                send(side, 6, 7, chunk, partner)
        visit(6, 7)
        for chunk in range(CHUNKS):
            for side in (IMAGE, TEXT):
                arrived(side, 7, chunk)
        visit(7, 8)
    else:
        for slot in range(1, 2 * WINDOW):
            for chunk in range(CHUNKS):
                for side in (IMAGE, TEXT):
                    arrived(side, slot, chunk)
        visit(1, 2 * WINDOW)

    outs = {IMAGE: grad_images_ref, TEXT: grad_texts_ref}
    for side in (IMAGE, TEXT):
        for chunk in range(CHUNKS):
            unit, inverse = normalize(sources[side][part(chunk), :])
            outs[side][part(chunk), :] = unit_backward(unit, inverse, grads[side, part(chunk), :])
    for copy in started:
        copy.wait_send()


def shards(images, texts, labels, log_scale, bias):
    rows, depth = images.shape
    wide_count = lax.axis_size("wide")
    narrow_count = lax.axis_size("narrow")
    vmem = pl.BlockSpec(memory_space=pltpu.VMEM)
    smem = pl.BlockSpec(memory_space=pltpu.SMEM)
    out = jax.ShapeDtypeStruct((rows, depth), jnp.float32)
    pairs = 2 * 2 * WINDOW * rows * rows
    return pl.pallas_call(
        functools.partial(kernel, wide_count, narrow_count),
        out_shape=(out, out),
        in_specs=[smem, smem, vmem, vmem, vmem],
        out_specs=(vmem, vmem),
        scratch_shapes=[
            pltpu.VMEM((2, 2 * WINDOW, rows, depth), jnp.bfloat16),
            pltpu.VMEM((2, rows, depth), jnp.float32),
            pltpu.SemaphoreType.DMA((2, 2 * WINDOW, CHUNKS)),
            pltpu.SemaphoreType.DMA((2, 2 * WINDOW, CHUNKS)),
        ],
        compiler_params=pltpu.CompilerParams(
            collective_id=0, has_side_effects=True, vmem_limit_bytes=40 * 1024 * 1024
        ),
        cost_estimate=pl.CostEstimate(
            flops=4 * pairs * depth, bytes_accessed=12 * rows * depth, transcendentals=pairs
        ),
        name="window_grads",
    )(log_scale, bias, images, texts, labels.reshape(1, rows))


def solution(mesh):
    return jax.shard_map(
        shards,
        mesh=mesh,
        in_specs=(
            P(("wide", "narrow"), None),
            P(("wide", "narrow"), None),
            P(("wide", "narrow")),
            P(),
            P(),
        ),
        out_specs=(P(("wide", "narrow"), None), P(("wide", "narrow"), None)),
        check_vma=False,
    )
```

time: 253 us -> 63.9 us (0.25)
  the two profiles are of different devices: /device:TPU:0 before, /device:TPU:7 now
where the time goes in v1:
time: 63.9 us; the launch traced here: 63.7 us
  Pallas kernels  56.9 us (89%)
  local copies, waits for them, and re-layouts  4.83 us (8%)
  between operations  1.94 us (3%)
    pallas_call x1, Pallas kernels, shards(): pl.pallas_call(functools.partial(kernel, wide_count, narrow_count), out_s...  56.9 us
    unnamed x8, local copies, waits for them, and re-layouts  4.83 us

profile of v1, /device:TPU:7, one launch (start us, length us, event | category | flops | bytes accessed | tf_op | source)
XLA Modules:
  0.0 63.7 jit_solution(14340117558406025515)
XLA Ops:
  1.9 0.0 copy-start
  1.9 1.1 %copy-done = bf16[256,1152]{1,0:T(8,128)(2,1)S(1)} copy-done((bf16[256,1152]{1,0:T(8,128)(2,1)S(1)}, bf16[256,1152]{1,0:T(8,128)(2,1)}, u32[]{:S(2)}) %copy-start) | copy-done | bytes 589848
  3.0 0.0 copy-start.1
  3.0 1.1 %copy-done.1 = bf16[256,1152]{1,0:T(8,128)(2,1)S(1)} copy-done((bf16[256,1152]{1,0:T(8,128)(2,1)S(1)}, bf16[256,1152]{1,0:T(8,128)(2,1)}, u32[]{:S(2)}) %copy-start.1) | copy-done | bytes 589848
  4.1 0.0 copy-start.2
  4.1 0.7 %copy-done.2 = s32[256]{0:T(256)S(1)} copy-done((s32[256]{0:T(256)S(1)}, s32[256]{0:T(256)}, u32[]{:S(2)}) %copy-start.2) | copy-done | bytes 1048
  4.7 56.9 %window_grads.1 = (f32[256,1152]{1,0:T(8,128)S(1)}, f32[256,1152]{1,0:T(8,128)S(1)}) custom-call(f32[1]{0:T(128)S(6)} %copy.9.log_scale_ref, f32[1]{0:T(128)S(6)} %copy.10.bias_ref, bf16[256,1152]{1,0:T(8,128)(2,1)S(1)} %copy-done, bf16[256,1152]{1,0:T(8,128)(2,1)S(1)} %copy-done.1, s32[1,256]{1,0:T(1,128)S(1)} %bitcast.1), custom_call_target="tpu_custom_call" | custom-call | flops 4831838208 | bytes 3538944 | tf_op jit(solution)/shard_map/window_grads/pallas_call | solution.py:192
  61.7 1.0 %copy.11 = f32[256,1152]{1,0:T(8,128)} copy(f32[256,1152]{1,0:T(8,128)S(1)} %get-tuple-element.4) | data formatting | bytes 2359296
  62.7 1.0 %copy.12 = f32[256,1152]{1,0:T(8,128)} copy(f32[256,1152]{1,0:T(8,128)S(1)} %get-tuple-element.5) | data formatting | bytes 2359296
Async XLA Ops:
  1.9 1.1 %copy-start = (bf16[256,1152]{1,0:T(8,128)(2,1)S(1)}, bf16[256,1152]{1,0:T(8,128)(2,1)}, u32[]{:S(2)}) copy-start(bf16[256,1152]{1,0:T(8,128)(2,1)} %images_ref.1) | copy-start | bytes 1769476
  3.0 1.1 %copy-start.1 = (bf16[256,1152]{1,0:T(8,128)(2,1)S(1)}, bf16[256,1152]{1,0:T(8,128)(2,1)}, u32[]{:S(2)}) copy-start(bf16[256,1152]{1,0:T(8,128)(2,1)} %texts_ref.1) | copy-start | bytes 1769476
  4.1 0.7 %copy-start.2 = (s32[256]{0:T(256)S(1)}, s32[256]{0:T(256)}, u32[]{:S(2)}) copy-start(s32[256]{0:T(256)} %param.7) | copy-start | bytes 3076

commit v2 on v1

v2 whole, which is shorter than its diff:
```python
import functools

import jax
import jax.numpy as jnp
from jax import lax
from jax.experimental import pallas as pl
from jax.experimental.pallas import tpu as pltpu
from jax.sharding import PartitionSpec as P

WINDOW = 4
EPS = 1e-06
CHUNKS = 4
MESH = pl.DeviceIdType.MESH


def normalize(vectors):
    floats = vectors.astype(jnp.float32)
    inverse = lax.rsqrt(jnp.sum(floats * floats, axis=-1, keepdims=True) + EPS)
    return (floats * inverse, inverse)


def unit_backward(unit_rows, inverse, upstream):
    return inverse * (upstream - unit_rows * jnp.sum(unit_rows * upstream, axis=-1, keepdims=True))


def kernel(
    wide_count,
    narrow_count,
    log_scale_ref,
    bias_ref,
    images_ref,
    texts_ref,
    labels_ref,
    grad_images_ref,
    grad_texts_ref,
    raw,
    labels_row,
    blocks,
    grads,
    load_sem,
    send_sem,
    recv_sem,
):
    rows = blocks.shape[2]
    piece = rows // CHUNKS
    wide = lax.axis_index("wide")
    narrow = lax.axis_index("narrow")
    relay = narrow_count == WINDOW and wide_count % 2 == 0
    odd = lax.rem(wide, 2)
    text_side = odd if relay else 0
    image_side = 1 - text_side

    def device(wide_step, narrow_index):
        return (lax.rem(wide + wide_step + wide_count, wide_count), narrow_index)

    if relay:
        partner = device(0, narrow + 1 - 2 * lax.rem(narrow, 2))
        across = device(0, lax.rem(narrow + 2, narrow_count))
        near = device(1 - 2 * odd, narrow)
        far = device(2 * odd - 1, narrow)
        neighbours = [partner, across, near, far]
    else:
        direct = {}
        for side, sign in ((0, 1), (1, -1)):
            for slot in range(1, 2 * WINDOW):
                wide_back = slot // WINDOW
                narrow_back = slot - wide_back * WINDOW + wide_back * (WINDOW - 1)
                index = lax.rem(narrow + sign * narrow_back + 2 * narrow_count, narrow_count)
                direct[side, slot] = device(sign * wide_back, index)
        neighbours = list(direct.values())

    loads = [
        pltpu.make_async_copy(images_ref, raw.at[image_side], load_sem.at[0]),
        pltpu.make_async_copy(texts_ref, raw.at[text_side], load_sem.at[1]),
        pltpu.make_async_copy(labels_ref, labels_row, load_sem.at[2]),
    ]
    for load in loads:
        load.start()
    barrier = pltpu.get_barrier_semaphore()
    for neighbour in neighbours:
        pl.semaphore_signal(barrier, inc=1, device_id=neighbour, device_id_type=MESH)

    temper = jnp.exp(jnp.full((1, rows), log_scale_ref[0], jnp.float32))
    offset = bias_ref[0]
    started = []

    def part(chunk):
        return pl.ds(chunk * piece, piece)

    def message(side, source_slot, to_side, slot, chunk, target):
        return pltpu.make_async_remote_copy(
            src_ref=blocks.at[side, source_slot, part(chunk)],
            dst_ref=blocks.at[to_side, slot, part(chunk)],
            send_sem=send_sem.at[to_side, slot, chunk],
            recv_sem=recv_sem.at[to_side, slot, chunk],
            device_id=target,
            device_id_type=MESH,
        )

    def send(side, source_slot, to_side, slot, chunk, target):
        copy = message(side, source_slot, to_side, slot, chunk, target)
        copy.start()
        started.append(copy)

    def arrived(side, slot, chunk):
        message(side, slot, side, slot, chunk, neighbours[0]).wait_recv()

    def all_arrived(slot):
        for chunk in range(CHUNKS):
            for side in (0, 1):
                arrived(side, slot, chunk)

    for load in loads:
        load.wait()
    for side in (0, 1):
        for chunk in range(CHUNKS):
            unit, _ = normalize(raw[side, part(chunk), :])
            blocks[side, 0, part(chunk), :] = unit.astype(jnp.bfloat16)
            if side == 0 and chunk == 0:
                pl.semaphore_wait(barrier, len(neighbours))
            if relay:
                send(side, 0, side, 2, chunk, across)
                send(side, 0, 1 - side, 4, chunk, far if side else near)
                send(side, 0, side, 1, chunk, partner)
            else:
                for slot in range(1, 2 * WINDOW):
                    send(side, 0, side, slot, chunk, direct[side, slot])

    def probability(own, visitor):
        scores = lax.dot_general(
            own, visitor, (((1,), (1,)), ((), ())), preferred_element_type=jnp.float32
        )
        return jax.nn.sigmoid(temper[:, : scores.shape[1]] * scores + offset)

    base = (wide * narrow_count + narrow) * rows
    target = base + lax.broadcasted_iota(jnp.int32, (rows, rows), 0)
    positive = (labels_row[...] == target).astype(jnp.float32)
    residual = probability(blocks[text_side, 0], blocks[image_side, 0]) - positive
    weighted = (temper * residual).astype(jnp.bfloat16)
    grads[text_side] = jnp.dot(weighted, blocks[image_side, 0], preferred_element_type=jnp.float32)
    grads[image_side] = lax.dot_general(
        weighted, blocks[text_side, 0], (((0,), (0,)), ((), ())), preferred_element_type=jnp.float32
    )

    def visit(first, last, start=0, count=rows):
        @pl.loop(0, 2 * (last - first))
        def _(step):
            side = lax.rem(step, 2)
            own = 1 - side
            visitor = blocks[side, first + step // 2, pl.ds(start, count), :]
            weighted = (temper[:, :count] * probability(blocks[own, 0], visitor)).astype(jnp.bfloat16)
            grads[own] += jnp.dot(weighted, visitor, preferred_element_type=jnp.float32)

    if relay:
        all_arrived(1)
        visit(1, 2)
        for chunk in range(CHUNKS):
            arrived(0, 2, chunk)
            send(0, 2, 1, 6, chunk, near)
            send(0, 2, 0, 3, chunk, partner)
            arrived(0, 4, chunk)
            send(0, 4, 0, 6, chunk, across)
            send(0, 4, 0, 5, chunk, partner)
            arrived(1, 4, chunk)
            send(1, 4, 1, 5, chunk, partner)
        all_arrived(5)
        visit(4, 6)
        for chunk in range(CHUNKS):
            arrived(1, 2, chunk)
            send(1, 2, 1, 3, chunk, partner)
        all_arrived(3)
        visit(2, 4)
        half = CHUNKS // 2
        for first in (0, half):
            for chunk in range(first, first + half):
                for side in (0, 1):
                    arrived(side, 6, chunk)
                    send(side, 6, side, 7, chunk, partner)
            visit(6, 7, first * piece, half * piece)
            for chunk in range(first, first + half):
                for side in (0, 1):
                    arrived(side, 7, chunk)
            visit(7, 8, first * piece, half * piece)
    else:
        for slot in range(1, 2 * WINDOW):
            all_arrived(slot)
        visit(1, 2 * WINDOW)

    for out, side in ((grad_images_ref, image_side), (grad_texts_ref, text_side)):
        for chunk in range(CHUNKS):
            unit, inverse = normalize(raw[side, part(chunk), :])
            out[part(chunk), :] = unit_backward(unit, inverse, grads[side, part(chunk), :])
    for copy in started:
        copy.wait_send()


def shards(images, texts, labels, log_scale, bias):
    rows, depth = images.shape
    wide_count = lax.axis_size("wide")
    narrow_count = lax.axis_size("narrow")
    vmem = pl.BlockSpec(memory_space=pltpu.VMEM)
    anywhere = pl.BlockSpec(memory_space=pl.ANY)
    smem = pl.BlockSpec(memory_space=pltpu.SMEM)
    out = jax.ShapeDtypeStruct((rows, depth), jnp.float32)
    pairs = 2 * 2 * WINDOW * rows * rows
    return pl.pallas_call(
        functools.partial(kernel, wide_count, narrow_count),
        out_shape=(out, out),
        in_specs=[smem, smem, anywhere, anywhere, anywhere],
        out_specs=(vmem, vmem),
        scratch_shapes=[
            pltpu.VMEM((2, rows, depth), images.dtype),
            pltpu.VMEM((1, rows), jnp.int32),
            pltpu.VMEM((2, 2 * WINDOW, rows, depth), jnp.bfloat16),
            pltpu.VMEM((2, rows, depth), jnp.float32),
            pltpu.SemaphoreType.DMA((3,)),
            pltpu.SemaphoreType.DMA((2, 2 * WINDOW, CHUNKS)),
            pltpu.SemaphoreType.DMA((2, 2 * WINDOW, CHUNKS)),
        ],
        compiler_params=pltpu.CompilerParams(
            collective_id=0, has_side_effects=True, vmem_limit_bytes=40 * 1024 * 1024
        ),
        cost_estimate=pl.CostEstimate(
            flops=4 * pairs * depth, bytes_accessed=12 * rows * depth, transcendentals=pairs
        ),
        name="window_grads",
    )(log_scale, bias, images, texts, labels.reshape(1, rows))


def solution(mesh):
    return jax.shard_map(
        shards,
        mesh=mesh,
        in_specs=(
            P(("wide", "narrow"), None),
            P(("wide", "narrow"), None),
            P(("wide", "narrow")),
            P(),
            P(),
        ),
        out_specs=(P(("wide", "narrow"), None), P(("wide", "narrow"), None)),
        check_vma=False,
    )
```

time: 63.9 us -> 58.2 us (0.911)
  the two profiles are of different devices: /device:TPU:7 before, /device:TPU:0 now
where the time goes in v2:
time: 58.2 us; the launch traced here: 57.9 us
  Pallas kernels  51.2 us (88%)
  local copies, waits for them, and re-layouts  4.83 us (8%)
  between operations  1.94 us (3%)
    pallas_call x1, Pallas kernels, shards(): pl.pallas_call(functools.partial(kernel, wide_count, narrow_count), out_s...  51.2 us
    unnamed x8, local copies, waits for them, and re-layouts  4.83 us

profile of v2, /device:TPU:0, one launch (start us, length us, event | category | flops | bytes accessed | tf_op | source)
XLA Modules:
  0.0 57.9 jit_solution(10589558089162072447)
XLA Ops:
  1.9 0.0 copy-start
  1.9 1.1 %copy-done = bf16[256,1152]{1,0:T(8,128)(2,1)S(1)} copy-done((bf16[256,1152]{1,0:T(8,128)(2,1)S(1)}, bf16[256,1152]{1,0:T(8,128)(2,1)}, u32[]{:S(2)}) %copy-start) | copy-done | bytes 589848
  3.0 0.0 copy-start.1
  3.0 1.1 %copy-done.1 = bf16[256,1152]{1,0:T(8,128)(2,1)S(1)} copy-done((bf16[256,1152]{1,0:T(8,128)(2,1)S(1)}, bf16[256,1152]{1,0:T(8,128)(2,1)}, u32[]{:S(2)}) %copy-start.1) | copy-done | bytes 589848
  4.1 0.0 copy-start.2
  4.1 0.7 %copy-done.2 = s32[256]{0:T(256)S(1)} copy-done((s32[256]{0:T(256)S(1)}, s32[256]{0:T(256)}, u32[]{:S(2)}) %copy-start.2) | copy-done | bytes 1048
  4.7 51.2 %window_grads.1 = (f32[256,1152]{1,0:T(8,128)S(1)}, f32[256,1152]{1,0:T(8,128)S(1)}) custom-call(f32[1]{0:T(128)S(6)} %copy.9.log_scale_ref, f32[1]{0:T(128)S(6)} %copy.10.bias_ref, bf16[256,1152]{1,0:T(8,128)(2,1)S(1)} %copy-done, bf16[256,1152]{1,0:T(8,128)(2,1)S(1)} %copy-done.1, s32[1,256]{1,0:T(1,128)S(1)} %bitcast.1), custom_call_target="tpu_custom_call" | custom-call | flops 4831838208 | bytes 3538944 | tf_op jit(solution)/shard_map/window_grads/pallas_call | solution.py:206
  55.9 1.0 %copy.11 = f32[256,1152]{1,0:T(8,128)} copy(f32[256,1152]{1,0:T(8,128)S(1)} %get-tuple-element.4) | data formatting | bytes 2359296
  56.9 1.0 %copy.12 = f32[256,1152]{1,0:T(8,128)} copy(f32[256,1152]{1,0:T(8,128)S(1)} %get-tuple-element.5) | data formatting | bytes 2359296
Async XLA Ops:
  1.9 1.1 %copy-start = (bf16[256,1152]{1,0:T(8,128)(2,1)S(1)}, bf16[256,1152]{1,0:T(8,128)(2,1)}, u32[]{:S(2)}) copy-start(bf16[256,1152]{1,0:T(8,128)(2,1)} %images_ref.1) | copy-start | bytes 1769476
  3.0 1.1 %copy-start.1 = (bf16[256,1152]{1,0:T(8,128)(2,1)S(1)}, bf16[256,1152]{1,0:T(8,128)(2,1)}, u32[]{:S(2)}) copy-start(bf16[256,1152]{1,0:T(8,128)(2,1)} %texts_ref.1) | copy-start | bytes 1769476
  4.1 0.7 %copy-start.2 = (s32[256]{0:T(256)S(1)}, s32[256]{0:T(256)}, u32[]{:S(2)}) copy-start(s32[256]{0:T(256)} %param.7) | copy-start | bytes 3076

commit v3 on v0

v3 whole, which is shorter than its diff:
```python
import functools

import jax
import jax.numpy as jnp
from jax import lax
from jax.experimental import pallas as pl
from jax.experimental.pallas import tpu as pltpu
from jax.sharding import PartitionSpec as P

WINDOW = 4
EPS = 1e-06
CHUNKS = 4
MESH = pl.DeviceIdType.MESH


def normalize(vectors):
    floats = vectors.astype(jnp.float32)
    inverse = lax.rsqrt(jnp.sum(floats * floats, axis=-1, keepdims=True) + EPS)
    return (floats * inverse, inverse)


def unit_backward(unit_rows, inverse, upstream):
    return inverse * (upstream - unit_rows * jnp.sum(unit_rows * upstream, axis=-1, keepdims=True))


def place(wide_count, wide_step, narrow_index):
    return (lax.rem(lax.axis_index("wide") + wide_step + wide_count, wide_count), narrow_index)


def greet(neighbours):
    barrier = pltpu.get_barrier_semaphore()
    for neighbour in neighbours:
        pl.semaphore_signal(barrier, inc=1, device_id=neighbour, device_id_type=MESH)
    return barrier


def probability(own, visitor, temper, offset):
    scores = lax.dot_general(
        own, visitor, (((1,), (1,)), ((), ())), preferred_element_type=jnp.float32
    )
    return jax.nn.sigmoid(temper * scores + offset)


def pull(own, visitor, temper, offset):
    weighted = (temper * probability(own, visitor, temper, offset)).astype(jnp.bfloat16)
    return jnp.dot(weighted, visitor, preferred_element_type=jnp.float32)


def own_pairs(image_rows, text_rows, labels_row, anchor, temper, offset):
    rows = image_rows.shape[0]
    target = anchor * rows + lax.broadcasted_iota(jnp.int32, (rows, rows), 0)
    positive = (labels_row == target).astype(jnp.float32)
    residual = probability(text_rows, image_rows, temper, offset) - positive
    weighted = (temper * residual).astype(jnp.bfloat16)
    image_grad = lax.dot_general(
        weighted, text_rows, (((0,), (0,)), ((), ())), preferred_element_type=jnp.float32
    )
    return image_grad, jnp.dot(weighted, image_rows, preferred_element_type=jnp.float32)


IMAGE, TEXT, IMAGE_ACROSS, TEXT_BACK = range(4)
I0, I1, I2, I3, T0, T1, T4, T5 = range(8)


def relay_kernel(
    wide_count,
    narrow_count,
    log_scale_ref,
    bias_ref,
    images_ref,
    texts_ref,
    labels_ref,
    grad_images_ref,
    grad_texts_ref,
    raw,
    labels_row,
    blocks,
    grads,
    outbox,
    inbox,
    load_sem,
    send_sem,
    recv_sem,
    grad_send_sem,
    grad_recv_sem,
):
    rows = blocks.shape[1]
    piece = rows // CHUNKS
    half = CHUNKS // 2
    narrow = lax.axis_index("narrow")
    partner = place(wide_count, 0, narrow + 1 - 2 * lax.rem(narrow, 2))
    across = place(wide_count, 0, lax.rem(narrow + 2, narrow_count))
    forth = place(wide_count, 1, narrow)
    back = place(wide_count, -1, narrow)
    neighbours = [partner, across, forth, back]

    def part(chunk):
        return pl.ds(chunk * piece, piece)

    sources = ((I0, raw.at[IMAGE], images_ref), (T0, raw.at[TEXT], texts_ref))
    loads = [
        [
            pltpu.make_async_copy(ref.at[part(chunk)], target.at[part(chunk)], load_sem.at[number, chunk])
            for number, (_, target, ref) in enumerate(sources)
        ]
        for chunk in range(CHUNKS)
    ]
    for pair in loads:
        for load in pair:
            load.start()
    label_load = pltpu.make_async_copy(labels_ref, labels_row, load_sem.at[2, 0])
    label_load.start()
    barrier = greet(neighbours)

    temper = jnp.exp(jnp.full((1, 1), log_scale_ref[0], jnp.float32))
    offset = bias_ref[0]
    started = []

    def message(source, slot, chunk, target):
        return pltpu.make_async_remote_copy(
            src_ref=blocks.at[source, part(chunk)],
            dst_ref=blocks.at[slot, part(chunk)],
            send_sem=send_sem.at[slot, chunk],
            recv_sem=recv_sem.at[slot, chunk],
            device_id=target,
            device_id_type=MESH,
        )

    def send(source, slot, chunk, target):
        copy = message(source, slot, chunk, target)
        copy.start()
        started.append(copy)

    def arrived(slot, first=0, last=CHUNKS):
        for chunk in range(first, last):
            message(slot, slot, chunk, partner).wait_recv()

    def return_message(side, chunk):
        return pltpu.make_async_remote_copy(
            src_ref=outbox.at[side, part(chunk)],
            dst_ref=inbox.at[side, part(chunk)],
            send_sem=grad_send_sem.at[side, chunk],
            recv_sem=grad_recv_sem.at[side, chunk],
            device_id=back if side else across,
            device_id_type=MESH,
        )

    for chunk in range(CHUNKS):
        for load in loads[chunk]:
            load.wait()
        for slot, source, _ in sources:
            unit, _ = normalize(source[part(chunk), :])
            blocks[slot, part(chunk), :] = unit.astype(jnp.bfloat16)
        if chunk == 0:
            pl.semaphore_wait(barrier, len(neighbours))
        send(I0, I2, chunk, across)
        send(T0, T4, chunk, forth)
        send(I0, I1, chunk, partner)
        send(T0, T1, chunk, partner)

    span = half * piece

    def add(target, own, own_half, first, visitor_half=None, count=2, fresh=False):
        own_rows = slice(None) if own_half is None else pl.ds(own_half * span, span)
        visitor_rows = slice(None) if visitor_half is None else pl.ds(visitor_half * span, span)
        visitor = blocks[first : first + count, visitor_rows, :]
        visitor = visitor.reshape(visitor.shape[0] * visitor.shape[1], visitor.shape[2])
        value = pull(blocks[own, own_rows, :], visitor, temper, offset)
        grads[target, own_rows, :] = value if fresh else grads[target, own_rows, :] + value

    def give(side, own_half):
        target = TEXT_BACK if side else IMAGE_ACROSS
        for chunk in range(own_half * half, (own_half + 1) * half):
            outbox[side, part(chunk), :] = grads[target, part(chunk), :].astype(outbox.dtype)
            copy = return_message(side, chunk)
            copy.start()
            started.append(copy)

    label_load.wait()
    anchor = lax.axis_index("wide") * narrow_count + narrow
    grads[IMAGE], grads[TEXT] = own_pairs(
        blocks[I0], blocks[T0], labels_row[...], anchor, temper, offset
    )
    arrived(I1)
    arrived(T1)
    add(IMAGE, I0, None, T1, count=1)
    add(TEXT, T0, None, I1, count=1)

    for turn in (0, 1):
        for chunk in range(turn * half, (turn + 1) * half):
            arrived(I2, chunk, chunk + 1)
            send(I2, I3, chunk, partner)
            arrived(T4, chunk, chunk + 1)
            send(T4, T5, chunk, partner)
        add(IMAGE_ACROSS, I2, turn, T0, fresh=True)
        add(TEXT_BACK, T4, turn, I0, fresh=True)
        arrived(T5, turn * half, (turn + 1) * half)
        add(IMAGE_ACROSS, I2, 0, T4, turn)
        if turn == 1:
            give(IMAGE, 0)
        arrived(I3, turn * half, (turn + 1) * half)
        add(TEXT_BACK, T4, 0, I2, turn)
        if turn == 1:
            give(TEXT, 0)
    add(IMAGE_ACROSS, I2, 1, T4)
    give(IMAGE, 1)
    add(TEXT_BACK, T4, 1, I2)
    give(TEXT, 1)
    add(IMAGE, I0, None, T4)
    add(TEXT, T0, None, I2)

    stores = []
    for chunk in range(CHUNKS):
        for side, out in ((IMAGE, grad_images_ref), (TEXT, grad_texts_ref)):
            return_message(side, chunk).wait_recv()
            unit, inverse = normalize(raw[side, part(chunk), :])
            total = grads[side, part(chunk), :] + inbox[side, part(chunk), :].astype(jnp.float32)
            grads[side, part(chunk), :] = unit_backward(unit, inverse, total)
            stores.append(
                pltpu.make_async_copy(grads.at[side, part(chunk)], out.at[part(chunk)], load_sem.at[side, chunk])
            )
            stores[-1].start()
    for copy in started:
        copy.wait_send()
    for store in stores:
        store.wait()


def direct_kernel(
    wide_count,
    narrow_count,
    log_scale_ref,
    bias_ref,
    images_ref,
    texts_ref,
    labels_ref,
    grad_images_ref,
    grad_texts_ref,
    labels_row,
    blocks,
    grads,
    load_sem,
    send_sem,
    recv_sem,
):
    rows = blocks.shape[2]
    wide = lax.axis_index("wide")
    narrow = lax.axis_index("narrow")
    slots = 2 * WINDOW
    targets = {}
    for side, sign in ((IMAGE, -1), (TEXT, 1)):
        for slot in range(1, slots):
            wide_back = slot // WINDOW
            narrow_back = slot - wide_back * WINDOW + wide_back * (WINDOW - 1)
            index = lax.rem(narrow + sign * narrow_back + 2 * narrow_count, narrow_count)
            targets[side, slot] = place(wide_count, sign * wide_back, index)
    load = pltpu.make_async_copy(labels_ref, labels_row, load_sem.at[0])
    load.start()
    barrier = greet(targets.values())

    temper = jnp.exp(jnp.full((1, 1), log_scale_ref[0], jnp.float32))
    offset = bias_ref[0]
    sources = {IMAGE: images_ref, TEXT: texts_ref}
    for side in (IMAGE, TEXT):
        blocks[side, 0] = normalize(sources[side][...])[0].astype(jnp.bfloat16)
    pl.semaphore_wait(barrier, len(targets))
    copies = {}
    for slot in range(1, slots):
        for side in (IMAGE, TEXT):
            copies[side, slot] = pltpu.make_async_remote_copy(
                src_ref=blocks.at[side, 0],
                dst_ref=blocks.at[side, slot],
                send_sem=send_sem.at[side, slot],
                recv_sem=recv_sem.at[side, slot],
                device_id=targets[side, slot],
                device_id_type=MESH,
            )
            copies[side, slot].start()
    load.wait()
    grads[IMAGE], grads[TEXT] = own_pairs(
        blocks[IMAGE, 0], blocks[TEXT, 0], labels_row[...], wide * narrow_count + narrow, temper, offset
    )
    for copy in copies.values():
        copy.wait_recv()

    @pl.loop(2, 2 * slots)
    def _(step):
        side = lax.rem(step, 2)
        grads[1 - side] += pull(blocks[1 - side, 0], blocks[side, step // 2], temper, offset)

    for side, out in ((IMAGE, grad_images_ref), (TEXT, grad_texts_ref)):
        unit, inverse = normalize(sources[side][...])
        out[...] = unit_backward(unit, inverse, grads[side])
    for copy in copies.values():
        copy.wait_send()


def shards(images, texts, labels, log_scale, bias):
    rows, depth = images.shape
    wide_count = lax.axis_size("wide")
    narrow_count = lax.axis_size("narrow")
    vmem = pl.BlockSpec(memory_space=pltpu.VMEM)
    smem = pl.BlockSpec(memory_space=pltpu.SMEM)
    hbm = pl.BlockSpec(memory_space=pltpu.HBM)
    row = pltpu.VMEM((1, rows), jnp.int32)
    dma = pltpu.SemaphoreType.DMA
    out = jax.ShapeDtypeStruct((rows, depth), jnp.float32)
    pairs = 2 * 2 * WINDOW * rows * rows
    if narrow_count == WINDOW:
        body, held = relay_kernel, hbm
        scratch = [
            pltpu.VMEM((2, rows, depth), images.dtype),
            row,
            pltpu.VMEM((2 * WINDOW, rows, depth), jnp.bfloat16),
            pltpu.VMEM((4, rows, depth), jnp.float32),
            pltpu.VMEM((2, rows, depth), jnp.bfloat16),
            pltpu.VMEM((2, rows, depth), jnp.bfloat16),
            dma((3, CHUNKS)),
            dma((2 * WINDOW, CHUNKS)),
            dma((2 * WINDOW, CHUNKS)),
            dma((2, CHUNKS)),
            dma((2, CHUNKS)),
        ]
    else:
        body, held = direct_kernel, vmem
        scratch = [
            row,
            pltpu.VMEM((2, 2 * WINDOW, rows, depth), jnp.bfloat16),
            pltpu.VMEM((2, rows, depth), jnp.float32),
            dma((1,)),
            dma((2, 2 * WINDOW)),
            dma((2, 2 * WINDOW)),
        ]
    return pl.pallas_call(
        functools.partial(body, wide_count, narrow_count),
        out_shape=(out, out),
        in_specs=[smem, smem, held, held, hbm],
        out_specs=(held, held),
        scratch_shapes=scratch,
        compiler_params=pltpu.CompilerParams(
            collective_id=0, has_side_effects=True, vmem_limit_bytes=60 * 1024 * 1024
        ),
        cost_estimate=pl.CostEstimate(
            flops=4 * pairs * depth, bytes_accessed=12 * rows * depth, transcendentals=pairs
        ),
        name="window_grads",
    )(log_scale, bias, images, texts, labels.reshape(1, rows))


def solution(mesh):
    return jax.shard_map(
        shards,
        mesh=mesh,
        in_specs=(
            P(("wide", "narrow"), None),
            P(("wide", "narrow"), None),
            P(("wide", "narrow")),
            P(),
            P(),
        ),
        out_specs=(P(("wide", "narrow"), None), P(("wide", "narrow"), None)),
        check_vma=False,
    )
```

time: 253 us -> 45.1 us (0.18)
  waiting for transfers between devices: 197 us -> 0 us
  Pallas kernels: 0 us -> 39.5 us
  matrix products: 21.6 us -> 0 us
  starting transfers between devices: 17.6 us -> 0 us
  other arithmetic: 12.8 us -> 0 us
    ppermute x16 -> x0, waiting for transfers between devices: 197 us -> none  [shifted(): return lax.ppermute(value, axis, pairs)]
    pallas_call x0 -> x1, Pallas kernels: none -> 39.5 us  [shards(): pl.pallas_call(functools.partial(body, wide_count, narrow_count), out_sha...]
    dot_general x24 -> x0, matrix products: 21.6 us -> none  [the longest x8 8.7 us: weigh_block(): jnp.einsum('id,jd->ij', image_rows, text_rows, preferred_element_type=jnp...]
    ppermute x16 -> x0, starting transfers between devices: 17.6 us -> none  [shifted(): return lax.ppermute(value, axis, pairs)]
    add x14 -> x0, other arithmetic: 7.14 us -> none  [the longest x6 7.12 us: visit(): carried + jnp.einsum('ij,id->jd', weighted, image_half, preferred_element...]
    reduce_sum x3 -> x0, other arithmetic: 2.91 us -> none  [the longest x2 2.61 us: normalize(): inverse = lax.rsqrt(jnp.sum(floats * floats, axis=-1, keepdims=True) + EPS)]
    mul x2 -> x0, other arithmetic: 2.56 us -> none  [unit_backward(): inverse * (upstream - unit_rows * jnp.sum(unit_rows * upstream, axis=-1,...]
  transfers between devices with their start and end apart: 16 -> 0, of which waited for: 10 -> 0; matrix products, arithmetic and copies ran while one was open for 9% -> 0% of each run, Pallas kernels for 0% -> 0%
where the time goes in v3:
time: 45.1 us; the launch traced here: 44.9 us
  Pallas kernels  39.5 us (88%)
  local copies, waits for them, and re-layouts  3.47 us (8%)
  between operations  1.94 us (4%)
    pallas_call x1, Pallas kernels, shards(): pl.pallas_call(functools.partial(body, wide_count, narrow_count), out_sha...  39.5 us
    unnamed x4, local copies, waits for them, and re-layouts  3.47 us

profile of v3, /device:TPU:0, one launch (start us, length us, event | category | flops | bytes accessed | tf_op | source)
XLA Modules:
  0.0 44.9 jit_solution(6619457022781065806)
XLA Ops:
  1.9 39.5 %window_grads.1 = (f32[256,1152]{1,0:T(8,128)}, f32[256,1152]{1,0:T(8,128)}) custom-call(f32[1]{0:T(128)S(6)} %copy.9.log_scale_ref, f32[1]{0:T(128)S(6)} %copy.10.bias_ref, bf16[256,1152]{1,0:T(8,128)(2,1)} %images_ref.1, bf16[256,1152]{1,0:T(8,128)(2,1)} %texts_ref.1, s32[1,256]{1,0:T(1,128)} %bitcast.1), custom_call_target="tpu_custom_call" | custom-call | flops 4831838208 | bytes 3538944 | tf_op jit(solution)/shard_map/window_grads/pallas_call | solution.py:334
  41.4 0.0 copy-start
  41.4 2.5 %copy.11 = f32[256,1152]{1,0:T(8,128)} copy(f32[256,1152]{1,0:T(8,128)} %get-tuple-element.4) | data formatting | bytes 2359296
  43.9 0.0 copy-done
  43.9 1.0 %copy.12 = f32[256,1152]{1,0:T(8,128)} copy(f32[256,1152]{1,0:T(8,128)S(1)} %copy-done) | data formatting | bytes 2359296
Async XLA Ops:
  41.4 2.5 %copy-start = (f32[256,1152]{1,0:T(8,128)S(1)}, f32[256,1152]{1,0:T(8,128)}, u32[]{:S(2)}) copy-start(f32[256,1152]{1,0:T(8,128)} %get-tuple-element.5) | copy-start | bytes 3538948

commit v4 on v3

--- a/solution.py
+++ b/solution.py
@@ -209,19 +209,23 @@
     add(IMAGE, I0, None, T4)
     add(TEXT, T0, None, I2)
 
-    stores = []
     for chunk in range(CHUNKS):
         for side, out in ((IMAGE, grad_images_ref), (TEXT, grad_texts_ref)):
             return_message(side, chunk).wait_recv()
             unit, inverse = normalize(raw[side, part(chunk), :])
             total = grads[side, part(chunk), :] + inbox[side, part(chunk), :].astype(jnp.float32)
-            grads[side, part(chunk), :] = unit_backward(unit, inverse, total)
-            stores.append(
-                pltpu.make_async_copy(grads.at[side, part(chunk)], out.at[part(chunk)], load_sem.at[side, chunk])
-            )
-            stores[-1].start()
+            out[part(chunk), :] = unit_backward(unit, inverse, total)
     for copy in started:
         copy.wait_send()
+
+
+def store_kernel(images_from, texts_from, images_to, texts_to, store_sem):
+    stores = [
+        pltpu.make_async_copy(images_from, images_to, store_sem.at[0]),
+        pltpu.make_async_copy(texts_from, texts_to, store_sem.at[1]),
+    ]
+    for store in stores:
+        store.start()
     for store in stores:
         store.wait()
 
@@ -331,20 +335,32 @@
             dma((2, 2 * WINDOW)),
             dma((2, 2 * WINDOW)),
         ]
-    return pl.pallas_call(
+    arrays = (images, texts, labels.reshape(1, rows))
+    if held is hbm:
+        arrays = tuple(pltpu.with_memory_space_constraint(array, pltpu.HBM) for array in arrays)
+    grads = pl.pallas_call(
         functools.partial(body, wide_count, narrow_count),
         out_shape=(out, out),
         in_specs=[smem, smem, held, held, hbm],
-        out_specs=(held, held),
+        out_specs=(vmem, vmem),
         scratch_shapes=scratch,
         compiler_params=pltpu.CompilerParams(
-            collective_id=0, has_side_effects=True, vmem_limit_bytes=60 * 1024 * 1024
+            collective_id=0, has_side_effects=True, vmem_limit_bytes=40 * 1024 * 1024
         ),
         cost_estimate=pl.CostEstimate(
             flops=4 * pairs * depth, bytes_accessed=12 * rows * depth, transcendentals=pairs
         ),
         name="window_grads",
-    )(log_scale, bias, images, texts, labels.reshape(1, rows))
+    )(log_scale, bias, *arrays)
+    anywhere = pl.BlockSpec(memory_space=pl.ANY)
+    return pl.pallas_call(
+        store_kernel,
+        out_shape=(out, out),
+        in_specs=[anywhere, anywhere],
+        out_specs=(hbm, hbm),
+        scratch_shapes=[dma((2,))],
+        name="store",
+    )(*grads)
 
 
 def solution(mesh):

time: 45.1 us -> 116 us (2.57)
  Pallas kernels: 39.5 us -> 111 us
  local copies, waits for them, and re-layouts: 3.47 us -> 2.07 us
    pallas_call x0 -> x1, Pallas kernels: none -> 72.6 us  [shards(): pl.pallas_call(store_kernel, out_shape=(out, out), in_specs=[anywhere, an...]
    unnamed x4, local copies, waits for them, and re-layouts: 3.47 us -> 2.07 us
where the time goes in v4:
time: 116 us; the launch traced here: 115 us
  Pallas kernels  111 us (96%)
  local copies, waits for them, and re-layouts  2.07 us (2%)
  between operations  1.94 us (2%)
    pallas_call x1, Pallas kernels, shards(): pl.pallas_call(store_kernel, out_shape=(out, out), in_specs=[anywhere, an...  72.6 us
    pallas_call x1, Pallas kernels, shards(): pl.pallas_call(functools.partial(body, wide_count, narrow_count), out_sha...  38.8 us

profile of v4, /device:TPU:0, one launch (start us, length us, event | category | flops | bytes accessed | tf_op | source)
XLA Modules:
  0.0 115.4 jit_solution(15908712321020788205)
XLA Ops:
  1.9 38.8 %window_grads.1 = (f32[256,1152]{1,0:T(8,128)S(1)}, f32[256,1152]{1,0:T(8,128)S(1)}) custom-call(f32[1]{0:T(128)S(6)} %copy.7.log_scale_ref, f32[1]{0:T(128)S(6)} %copy.8.bias_ref, bf16[256,1152]{1,0:T(8,128)(2,1)} %images_ref.1, bf16[256,1152]{1,0:T(8,128)(2,1)} %texts_ref.1, s32[1,256]{1,0:T(1,128)} %bitcast.1), custom_call_target="tpu_custom_call" | custom-call | flops 4831838208 | bytes 3538944 | tf_op jit(solution)/shard_map/window_grads/pallas_call | solution.py:341
  40.7 0.0 copy-start
  40.7 1.0 copy-done
  41.8 0.0 copy-start.1
  41.8 1.1 copy-done.1
  42.8 72.6 %store.1 = (f32[256,1152]{1,0:T(8,128)}, f32[256,1152]{1,0:T(8,128)}) custom-call(f32[256,1152]{1,0:T(8,128)} %copy-done, f32[256,1152]{1,0:T(8,128)} %copy-done.1), custom_call_target="tpu_custom_call" | custom-call | tf_op jit(solution)/shard_map/store/pallas_call | solution.py:356
Async XLA Ops:
  40.7 1.0 copy-start
  41.8 1.1 copy-start.1

commit v5 on v3

--- a/solution.py
+++ b/solution.py
@@ -158,15 +158,20 @@
         send(I0, I1, chunk, partner)
         send(T0, T1, chunk, partner)
 
-    span = half * piece
-
-    def add(target, own, own_half, first, visitor_half=None, count=2, fresh=False):
-        own_rows = slice(None) if own_half is None else pl.ds(own_half * span, span)
-        visitor_rows = slice(None) if visitor_half is None else pl.ds(visitor_half * span, span)
-        visitor = blocks[first : first + count, visitor_rows, :]
+    def cut(half_or_all):
+        return slice(None) if half_or_all is None else pl.ds(half_or_all * half * piece, half * piece)
+
+    def add(target, own, own_half, first, rows_of_each=slice(None), count=2, fresh=False):
+        visitor = blocks[first : first + count, rows_of_each, :]
         visitor = visitor.reshape(visitor.shape[0] * visitor.shape[1], visitor.shape[2])
-        value = pull(blocks[own, own_rows, :], visitor, temper, offset)
-        grads[target, own_rows, :] = value if fresh else grads[target, own_rows, :] + value
+        value = pull(blocks[own, cut(own_half), :], visitor, temper, offset)
+        grads[target, cut(own_half), :] = value if fresh else grads[target, cut(own_half), :] + value
+
+    def pass_on(chunk):
+        arrived(T4, chunk, chunk + 1)
+        send(T4, T5, chunk, partner)
+        arrived(I2, chunk, chunk + 1)
+        send(I2, I3, chunk, partner)
 
     def give(side, own_half):
         target = TEXT_BACK if side else IMAGE_ACROSS
@@ -186,44 +191,38 @@
     add(IMAGE, I0, None, T1, count=1)
     add(TEXT, T0, None, I1, count=1)
 
-    for turn in (0, 1):
-        for chunk in range(turn * half, (turn + 1) * half):
-            arrived(I2, chunk, chunk + 1)
-            send(I2, I3, chunk, partner)
-            arrived(T4, chunk, chunk + 1)
-            send(T4, T5, chunk, partner)
-        add(IMAGE_ACROSS, I2, turn, T0, fresh=True)
-        add(TEXT_BACK, T4, turn, I0, fresh=True)
-        arrived(T5, turn * half, (turn + 1) * half)
-        add(IMAGE_ACROSS, I2, 0, T4, turn)
-        if turn == 1:
+    for chunk in range(half):
+        pass_on(chunk)
+    add(IMAGE_ACROSS, I2, 0, T0, fresh=True)
+    add(TEXT_BACK, T4, 0, I0, fresh=True)
+    arrived(T5, 0, half)
+    add(IMAGE_ACROSS, I2, 0, T4, cut(0))
+    arrived(I3, 0, half)
+    add(TEXT_BACK, T4, 0, I2, cut(0))
+    for chunk in range(half, CHUNKS):
+        pass_on(chunk)
+        arrived(T5, chunk, chunk + 1)
+        add(IMAGE_ACROSS, I2, 0, T4, part(chunk))
+        if chunk == CHUNKS - 1:
             give(IMAGE, 0)
-        arrived(I3, turn * half, (turn + 1) * half)
-        add(TEXT_BACK, T4, 0, I2, turn)
-        if turn == 1:
-            give(TEXT, 0)
-    add(IMAGE_ACROSS, I2, 1, T4)
+        arrived(I3, chunk, chunk + 1)
+        add(TEXT_BACK, T4, 0, I2, part(chunk))
+    give(TEXT, 0)
+    add(IMAGE_ACROSS, I2, 1, T0, count=4, fresh=True)
     give(IMAGE, 1)
-    add(TEXT_BACK, T4, 1, I2)
+    add(TEXT_BACK, T4, 1, I0, count=4, fresh=True)
     give(TEXT, 1)
     add(IMAGE, I0, None, T4)
     add(TEXT, T0, None, I2)
 
-    stores = []
     for chunk in range(CHUNKS):
         for side, out in ((IMAGE, grad_images_ref), (TEXT, grad_texts_ref)):
             return_message(side, chunk).wait_recv()
             unit, inverse = normalize(raw[side, part(chunk), :])
             total = grads[side, part(chunk), :] + inbox[side, part(chunk), :].astype(jnp.float32)
-            grads[side, part(chunk), :] = unit_backward(unit, inverse, total)
-            stores.append(
-                pltpu.make_async_copy(grads.at[side, part(chunk)], out.at[part(chunk)], load_sem.at[side, chunk])
-            )
-            stores[-1].start()
+            out[part(chunk), :] = unit_backward(unit, inverse, total)
     for copy in started:
         copy.wait_send()
-    for store in stores:
-        store.wait()
 
 
 def direct_kernel(
@@ -331,21 +330,23 @@
             dma((2, 2 * WINDOW)),
             dma((2, 2 * WINDOW)),
         ]
+    arrays = (images, texts, labels.reshape(1, rows))
+    if held is hbm:
+        arrays = tuple(pltpu.with_memory_space_constraint(array, pltpu.HBM) for array in arrays)
     return pl.pallas_call(
         functools.partial(body, wide_count, narrow_count),
         out_shape=(out, out),
         in_specs=[smem, smem, held, held, hbm],
-        out_specs=(held, held),
+        out_specs=(vmem, vmem),
         scratch_shapes=scratch,
         compiler_params=pltpu.CompilerParams(
-            collective_id=0, has_side_effects=True, vmem_limit_bytes=60 * 1024 * 1024
+            collective_id=0, has_side_effects=True, vmem_limit_bytes=40 * 1024 * 1024
         ),
         cost_estimate=pl.CostEstimate(
             flops=4 * pairs * depth, bytes_accessed=12 * rows * depth, transcendentals=pairs
         ),
         name="window_grads",
-    )(log_scale, bias, images, texts, labels.reshape(1, rows))
-
+    )(log_scale, bias, *arrays)
 
 def solution(mesh):
     return jax.shard_map(

time: 45.1 us -> 42.7 us (0.947)
  local copies, waits for them, and re-layouts: 3.47 us -> 2.03 us
  Pallas kernels: 39.5 us -> 38.6 us
    unnamed x4 -> x2, local copies, waits for them, and re-layouts: 3.47 us -> 2.03 us
    pallas_call x1, Pallas kernels: 39.5 us -> 38.6 us  [shards(): pl.pallas_call(functools.partial(body, wide_count, narrow_count), out_sha...]
where the time goes in v5:
time: 42.7 us; the launch traced here: 42.6 us
  Pallas kernels  38.6 us (90%)
  local copies, waits for them, and re-layouts  2.03 us (5%)
  between operations  1.93 us (5%)
    pallas_call x1, Pallas kernels, shards(): pl.pallas_call(functools.partial(body, wide_count, narrow_count), out_sha...  38.6 us
    unnamed x2, local copies, waits for them, and re-layouts  2.03 us

profile of v5, /device:TPU:0, one launch (start us, length us, event | category | flops | bytes accessed | tf_op | source)
XLA Modules:
  0.0 42.6 jit_solution(1149398370074733959)
XLA Ops:
  1.9 38.6 %window_grads.1 = (f32[256,1152]{1,0:T(8,128)S(1)}, f32[256,1152]{1,0:T(8,128)S(1)}) custom-call(f32[1]{0:T(128)S(6)} %copy.9.log_scale_ref, f32[1]{0:T(128)S(6)} %copy.10.bias_ref, bf16[256,1152]{1,0:T(8,128)(2,1)} %images_ref.1, bf16[256,1152]{1,0:T(8,128)(2,1)} %texts_ref.1, s32[1,256]{1,0:T(1,128)} %bitcast.1), custom_call_target="tpu_custom_call" | custom-call | flops 4831838208 | bytes 3538944 | tf_op jit(solution)/shard_map/window_grads/pallas_call | solution.py:336
  40.5 1.0 %copy.11 = f32[256,1152]{1,0:T(8,128)} copy(f32[256,1152]{1,0:T(8,128)S(1)} %get-tuple-element.4) | data formatting | bytes 2359296
  41.6 1.0 %copy.12 = f32[256,1152]{1,0:T(8,128)} copy(f32[256,1152]{1,0:T(8,128)S(1)} %get-tuple-element.5) | data formatting | bytes 2359296

commit v6 on v5

--- a/solution.py
+++ b/solution.py
@@ -9,7 +9,7 @@
 
 WINDOW = 4
 EPS = 1e-06
-CHUNKS = 4
+CHUNKS = 8
 MESH = pl.DeviceIdType.MESH
 
 

time: 42.7 us -> 45.6 us (1.068)
  Pallas kernels: 38.6 us -> 41.4 us
    pallas_call x1, Pallas kernels: 38.6 us -> 41.4 us  [shards(): pl.pallas_call(functools.partial(body, wide_count, narrow_count), out_sha...]
where the time goes in v6:
time: 45.6 us; the launch traced here: 45.4 us
  Pallas kernels  41.4 us (91%)
  local copies, waits for them, and re-layouts  2.03 us (4%)
  between operations  1.93 us (4%)
    pallas_call x1, Pallas kernels, shards(): pl.pallas_call(functools.partial(body, wide_count, narrow_count), out_sha...  41.4 us
    unnamed x2, local copies, waits for them, and re-layouts  2.03 us

profile of v6, /device:TPU:0, one launch (start us, length us, event | category | flops | bytes accessed | tf_op | source)
XLA Modules:
  0.0 45.4 jit_solution(17550181965895088877)
XLA Ops:
  1.9 41.4 %window_grads.1 = (f32[256,1152]{1,0:T(8,128)S(1)}, f32[256,1152]{1,0:T(8,128)S(1)}) custom-call(f32[1]{0:T(128)S(6)} %copy.9.log_scale_ref, f32[1]{0:T(128)S(6)} %copy.10.bias_ref, bf16[256,1152]{1,0:T(8,128)(2,1)} %images_ref.1, bf16[256,1152]{1,0:T(8,128)(2,1)} %texts_ref.1, s32[1,256]{1,0:T(1,128)} %bitcast.1), custom_call_target="tpu_custom_call" | custom-call | flops 4831838208 | bytes 3538944 | tf_op jit(solution)/shard_map/window_grads/pallas_call | solution.py:336
  43.4 1.0 %copy.11 = f32[256,1152]{1,0:T(8,128)} copy(f32[256,1152]{1,0:T(8,128)S(1)} %get-tuple-element.4) | data formatting | bytes 2359296
  44.4 1.0 %copy.12 = f32[256,1152]{1,0:T(8,128)} copy(f32[256,1152]{1,0:T(8,128)S(1)} %get-tuple-element.5) | data formatting | bytes 2359296

commit v7 on v5

--- a/solution.py
+++ b/solution.py
@@ -131,7 +131,17 @@
         copy.start()
         started.append(copy)
 
-    def arrived(slot, first=0, last=CHUNKS):
+    def whole(source, slot):
+        return pltpu.make_async_remote_copy(
+            src_ref=blocks.at[source],
+            dst_ref=blocks.at[slot],
+            send_sem=send_sem.at[slot, 0],
+            recv_sem=recv_sem.at[slot, 0],
+            device_id=partner,
+            device_id_type=MESH,
+        )
+
+    def arrived(slot, first, last):
         for chunk in range(first, last):
             message(slot, slot, chunk, partner).wait_recv()
 
@@ -155,8 +165,9 @@
             pl.semaphore_wait(barrier, len(neighbours))
         send(I0, I2, chunk, across)
         send(T0, T4, chunk, forth)
-        send(I0, I1, chunk, partner)
-        send(T0, T1, chunk, partner)
+    for slot, source in ((I1, I0), (T1, T0)):
+        started.append(whole(source, slot))
+        started[-1].start()
 
     def cut(half_or_all):
         return slice(None) if half_or_all is None else pl.ds(half_or_all * half * piece, half * piece)
@@ -186,8 +197,8 @@
     grads[IMAGE], grads[TEXT] = own_pairs(
         blocks[I0], blocks[T0], labels_row[...], anchor, temper, offset
     )
-    arrived(I1)
-    arrived(T1)
+    whole(I0, I1).wait_recv()
+    whole(T0, T1).wait_recv()
     add(IMAGE, I0, None, T1, count=1)
     add(TEXT, T0, None, I1, count=1)
 

time: 42.7 us -> 42.7 us (level)
  no operation moved by 1% of the time
where the time goes in v7:
time: 42.7 us; the launch traced here: 42.6 us
  Pallas kernels  38.6 us (90%)
  local copies, waits for them, and re-layouts  2.03 us (5%)
  between operations  1.93 us (5%)
    pallas_call x1, Pallas kernels, shards(): pl.pallas_call(functools.partial(body, wide_count, narrow_count), out_sha...  38.6 us
    unnamed x2, local copies, waits for them, and re-layouts  2.03 us

profile of v7, /device:TPU:0, one launch (start us, length us, event | category | flops | bytes accessed | tf_op | source)
XLA Modules:
  0.0 42.6 jit_solution(11808284221387467384)
XLA Ops:
  1.9 38.6 %window_grads.1 = (f32[256,1152]{1,0:T(8,128)S(1)}, f32[256,1152]{1,0:T(8,128)S(1)}) custom-call(f32[1]{0:T(128)S(6)} %copy.9.log_scale_ref, f32[1]{0:T(128)S(6)} %copy.10.bias_ref, bf16[256,1152]{1,0:T(8,128)(2,1)} %images_ref.1, bf16[256,1152]{1,0:T(8,128)(2,1)} %texts_ref.1, s32[1,256]{1,0:T(1,128)} %bitcast.1), custom_call_target="tpu_custom_call" | custom-call | flops 4831838208 | bytes 3538944 | tf_op jit(solution)/shard_map/window_grads/pallas_call | solution.py:347
  40.5 1.0 %copy.11 = f32[256,1152]{1,0:T(8,128)} copy(f32[256,1152]{1,0:T(8,128)S(1)} %get-tuple-element.4) | data formatting | bytes 2359296
  41.6 1.0 %copy.12 = f32[256,1152]{1,0:T(8,128)} copy(f32[256,1152]{1,0:T(8,128)S(1)} %get-tuple-element.5) | data formatting | bytes 2359296

commit v8 on v7

--- a/solution.py
+++ b/solution.py
@@ -184,13 +184,20 @@
         arrived(I2, chunk, chunk + 1)
         send(I2, I3, chunk, partner)
 
-    def give(side, own_half):
-        target = TEXT_BACK if side else IMAGE_ACROSS
+    def last_adds(own_half, rows_of_each, first_image, first_text, count, fresh):
+        totals = []
+        for target, own, first in ((IMAGE_ACROSS, I2, first_text), (TEXT_BACK, T4, first_image)):
+            visitor = blocks[first : first + count, rows_of_each, :]
+            visitor = visitor.reshape(visitor.shape[0] * visitor.shape[1], visitor.shape[2])
+            value = pull(blocks[own, cut(own_half), :], visitor, temper, offset)
+            totals.append(value if fresh else grads[target, cut(own_half), :] + value)
+        for side, total in enumerate(totals):
+            outbox[side, cut(own_half), :] = total.astype(outbox.dtype)
         for chunk in range(own_half * half, (own_half + 1) * half):
-            outbox[side, part(chunk), :] = grads[target, part(chunk), :].astype(outbox.dtype)
-            copy = return_message(side, chunk)
-            copy.start()
-            started.append(copy)
+            for side in (IMAGE, TEXT):
+                copy = return_message(side, chunk)
+                copy.start()
+                started.append(copy)
 
     label_load.wait()
     anchor = lax.axis_index("wide") * narrow_count + narrow
@@ -213,16 +220,12 @@
     for chunk in range(half, CHUNKS):
         pass_on(chunk)
         arrived(T5, chunk, chunk + 1)
-        add(IMAGE_ACROSS, I2, 0, T4, part(chunk))
-        if chunk == CHUNKS - 1:
-            give(IMAGE, 0)
         arrived(I3, chunk, chunk + 1)
-        add(TEXT_BACK, T4, 0, I2, part(chunk))
-    give(TEXT, 0)
-    add(IMAGE_ACROSS, I2, 1, T0, count=4, fresh=True)
-    give(IMAGE, 1)
-    add(TEXT_BACK, T4, 1, I0, count=4, fresh=True)
-    give(TEXT, 1)
+        if chunk < CHUNKS - 1:
+            add(IMAGE_ACROSS, I2, 0, T4, part(chunk))
+            add(TEXT_BACK, T4, 0, I2, part(chunk))
+    last_adds(0, part(CHUNKS - 1), I2, T4, 2, False)
+    last_adds(1, slice(None), I0, T0, 4, True)
     add(IMAGE, I0, None, T4)
     add(TEXT, T0, None, I2)
 

time: 42.7 us -> 43.2 us (1.012)
  Pallas kernels: 38.6 us -> 39.1 us
    pallas_call x1, Pallas kernels: 38.6 us -> 39.1 us  [shards(): pl.pallas_call(functools.partial(body, wide_count, narrow_count), out_sha...]
where the time goes in v8:
time: 43.2 us; the launch traced here: 43.1 us
  Pallas kernels  39.1 us (91%)
  local copies, waits for them, and re-layouts  2.03 us (5%)
  between operations  1.93 us (4%)
    pallas_call x1, Pallas kernels, shards(): pl.pallas_call(functools.partial(body, wide_count, narrow_count), out_sha...  39.1 us
    unnamed x2, local copies, waits for them, and re-layouts  2.03 us

profile of v8, /device:TPU:0, one launch (start us, length us, event | category | flops | bytes accessed | tf_op | source)
XLA Modules:
  0.0 43.1 jit_solution(4301128474212999188)
XLA Ops:
  1.9 39.1 %window_grads.1 = (f32[256,1152]{1,0:T(8,128)S(1)}, f32[256,1152]{1,0:T(8,128)S(1)}) custom-call(f32[1]{0:T(128)S(6)} %copy.9.log_scale_ref, f32[1]{0:T(128)S(6)} %copy.10.bias_ref, bf16[256,1152]{1,0:T(8,128)(2,1)} %images_ref.1, bf16[256,1152]{1,0:T(8,128)(2,1)} %texts_ref.1, s32[1,256]{1,0:T(1,128)} %bitcast.1), custom_call_target="tpu_custom_call" | custom-call | flops 4831838208 | bytes 3538944 | tf_op jit(solution)/shard_map/window_grads/pallas_call | solution.py:350
  41.0 1.0 %copy.11 = f32[256,1152]{1,0:T(8,128)} copy(f32[256,1152]{1,0:T(8,128)S(1)} %get-tuple-element.4) | data formatting | bytes 2359296
  42.1 1.0 %copy.12 = f32[256,1152]{1,0:T(8,128)} copy(f32[256,1152]{1,0:T(8,128)S(1)} %get-tuple-element.5) | data formatting | bytes 2359296

commit v9 on v7

--- a/solution.py
+++ b/solution.py
@@ -9,7 +9,7 @@
 
 WINDOW = 4
 EPS = 1e-06
-CHUNKS = 4
+CHUNKS = 2
 MESH = pl.DeviceIdType.MESH
 
 

time: 42.7 us -> 41.9 us (0.981)
  Pallas kernels: 38.6 us -> 37.8 us
    pallas_call x1, Pallas kernels: 38.6 us -> 37.8 us  [shards(): pl.pallas_call(functools.partial(body, wide_count, narrow_count), out_sha...]
where the time goes in v9:
time: 41.9 us; the launch traced here: 41.8 us
  Pallas kernels  37.8 us (90%)
  local copies, waits for them, and re-layouts  2.03 us (5%)
  between operations  1.93 us (5%)
    pallas_call x1, Pallas kernels, shards(): pl.pallas_call(functools.partial(body, wide_count, narrow_count), out_sha...  37.8 us
    unnamed x2, local copies, waits for them, and re-layouts  2.03 us

profile of v9, /device:TPU:0, one launch (start us, length us, event | category | flops | bytes accessed | tf_op | source)
XLA Modules:
  0.0 41.8 jit_solution(10251863429056657606)
XLA Ops:
  1.9 37.8 %window_grads.1 = (f32[256,1152]{1,0:T(8,128)S(1)}, f32[256,1152]{1,0:T(8,128)S(1)}) custom-call(f32[1]{0:T(128)S(6)} %copy.9.log_scale_ref, f32[1]{0:T(128)S(6)} %copy.10.bias_ref, bf16[256,1152]{1,0:T(8,128)(2,1)} %images_ref.1, bf16[256,1152]{1,0:T(8,128)(2,1)} %texts_ref.1, s32[1,256]{1,0:T(1,128)} %bitcast.1), custom_call_target="tpu_custom_call" | custom-call | flops 4831838208 | bytes 3538944 | tf_op jit(solution)/shard_map/window_grads/pallas_call | solution.py:347
  39.7 1.0 %copy.11 = f32[256,1152]{1,0:T(8,128)} copy(f32[256,1152]{1,0:T(8,128)S(1)} %get-tuple-element.4) | data formatting | bytes 2359296
  40.7 1.0 %copy.12 = f32[256,1152]{1,0:T(8,128)} copy(f32[256,1152]{1,0:T(8,128)S(1)} %get-tuple-element.5) | data formatting | bytes 2359296

commit v10 on v9

--- a/solution.py
+++ b/solution.py
@@ -172,25 +172,25 @@
     def cut(half_or_all):
         return slice(None) if half_or_all is None else pl.ds(half_or_all * half * piece, half * piece)
 
-    def add(target, own, own_half, first, rows_of_each=slice(None), count=2, fresh=False):
+    def add(target, own, own_half, first, rows_of_each=slice(None), count=2, fresh=False, leaving=None):
         visitor = blocks[first : first + count, rows_of_each, :]
         visitor = visitor.reshape(visitor.shape[0] * visitor.shape[1], visitor.shape[2])
         value = pull(blocks[own, cut(own_half), :], visitor, temper, offset)
-        grads[target, cut(own_half), :] = value if fresh else grads[target, cut(own_half), :] + value
+        total = value if fresh else grads[target, cut(own_half), :] + value
+        if leaving is None:
+            grads[target, cut(own_half), :] = total
+            return
+        outbox[leaving, cut(own_half), :] = total.astype(outbox.dtype)
+        for chunk in range(own_half * half, (own_half + 1) * half):
+            copy = return_message(leaving, chunk)
+            copy.start()
+            started.append(copy)
 
     def pass_on(chunk):
         arrived(T4, chunk, chunk + 1)
         send(T4, T5, chunk, partner)
         arrived(I2, chunk, chunk + 1)
         send(I2, I3, chunk, partner)
-
-    def give(side, own_half):
-        target = TEXT_BACK if side else IMAGE_ACROSS
-        for chunk in range(own_half * half, (own_half + 1) * half):
-            outbox[side, part(chunk), :] = grads[target, part(chunk), :].astype(outbox.dtype)
-            copy = return_message(side, chunk)
-            copy.start()
-            started.append(copy)
 
     label_load.wait()
     anchor = lax.axis_index("wide") * narrow_count + narrow
@@ -211,18 +211,14 @@
     arrived(I3, 0, half)
     add(TEXT_BACK, T4, 0, I2, cut(0))
     for chunk in range(half, CHUNKS):
+        last = chunk == CHUNKS - 1
         pass_on(chunk)
         arrived(T5, chunk, chunk + 1)
-        add(IMAGE_ACROSS, I2, 0, T4, part(chunk))
-        if chunk == CHUNKS - 1:
-            give(IMAGE, 0)
+        add(IMAGE_ACROSS, I2, 0, T4, part(chunk), leaving=IMAGE if last else None)
         arrived(I3, chunk, chunk + 1)
-        add(TEXT_BACK, T4, 0, I2, part(chunk))
-    give(TEXT, 0)
-    add(IMAGE_ACROSS, I2, 1, T0, count=4, fresh=True)
-    give(IMAGE, 1)
-    add(TEXT_BACK, T4, 1, I0, count=4, fresh=True)
-    give(TEXT, 1)
+        add(TEXT_BACK, T4, 0, I2, part(chunk), leaving=TEXT if last else None)
+    add(IMAGE_ACROSS, I2, 1, T0, count=4, fresh=True, leaving=IMAGE)
+    add(TEXT_BACK, T4, 1, I0, count=4, fresh=True, leaving=TEXT)
     add(IMAGE, I0, None, T4)
     add(TEXT, T0, None, I2)
 

time: 41.9 us -> 41.9 us (level)
  no operation moved by 1% of the time
where the time goes in v10:
time: 41.9 us; the launch traced here: 41.8 us
  Pallas kernels  37.8 us (90%)
  local copies, waits for them, and re-layouts  2.03 us (5%)
  between operations  1.93 us (5%)
    pallas_call x1, Pallas kernels, shards(): pl.pallas_call(functools.partial(body, wide_count, narrow_count), out_sha...  37.8 us
    unnamed x2, local copies, waits for them, and re-layouts  2.03 us

profile of v10, /device:TPU:0, one launch (start us, length us, event | category | flops | bytes accessed | tf_op | source)
XLA Modules:
  0.0 41.8 jit_solution(10251863429056657606)
XLA Ops:
  1.9 37.8 %window_grads.1 = (f32[256,1152]{1,0:T(8,128)S(1)}, f32[256,1152]{1,0:T(8,128)S(1)}) custom-call(f32[1]{0:T(128)S(6)} %copy.9.log_scale_ref, f32[1]{0:T(128)S(6)} %copy.10.bias_ref, bf16[256,1152]{1,0:T(8,128)(2,1)} %images_ref.1, bf16[256,1152]{1,0:T(8,128)(2,1)} %texts_ref.1, s32[1,256]{1,0:T(1,128)} %bitcast.1), custom_call_target="tpu_custom_call" | custom-call | flops 4831838208 | bytes 3538944 | tf_op jit(solution)/shard_map/window_grads/pallas_call | solution.py:343
  39.7 1.0 %copy.11 = f32[256,1152]{1,0:T(8,128)} copy(f32[256,1152]{1,0:T(8,128)S(1)} %get-tuple-element.4) | data formatting | bytes 2359296
  40.7 1.0 %copy.12 = f32[256,1152]{1,0:T(8,128)} copy(f32[256,1152]{1,0:T(8,128)S(1)} %get-tuple-element.5) | data formatting | bytes 2359296
